TPU v7x, 768 devices: a whole 4x8x12 slice. The times are simulated.
768 devices in a mesh: dp: 12 (over z), block: 64 (over y, x, core).
Axes of the slice: x: 4, y: 8, z: 12, core: 2. Of those that a mesh axis runs over, the one named last changes fastest.
Arguments:
- grad_part: bfloat16 [12, 192, 512, 512], P('dp', None, 'block'), may hold values from -1.796875 to 1.796875
- owner_table: int32 [192], P('dp'), may hold values from 0 to 63, as said below
- left_stats: bfloat16 [12, 64, 512, 512], P('dp', 'block'), may hold values from -16 to 16384, as said below
- right_stats: bfloat16 [12, 64, 512, 512], P('dp', 'block'), may hold values from -16 to 16384, as said below
Outputs:
- update: bfloat16 [192, 512, 512], P('dp', 'block')
Inputs may be any that keep to these rules, and one draw needn't show every extreme that they name: `owner_table`: within each group of 16 consecutive entries no owner is named twice. `left_stats`: every 512 x 512 matrix is symmetric and positive definite. `right_stats`: every 512 x 512 matrix is symmetric and positive definite.
All inputs are finite; a program needn't handle non-finite values. Where the computation divides by a largest or mean magnitude, that divisor is 1e-20 or more.
Results may differ from a plain program's by a relative error of at most 0.023.
Values may be sent and summed in bfloat16 or wider, within the bound.
A program may use at most 32 MiB of HBM per device.

v0:
```python
import jax
import jax.numpy as jnp
from jax import lax
from jax.sharding import PartitionSpec as P

DECAY = 0.9
EPSILON = 1e-06


def batched(pattern, left_side, right_side):
    return jnp.einsum(pattern, left_side, right_side, preferred_element_type=jnp.float32)


def inverse_root(statistic):
    row_bound = jnp.max(jnp.sum(jnp.abs(statistic), axis=-1), axis=-1)[..., None, None]
    scaled = statistic / row_bound
    scaled_low = scaled.astype(jnp.bfloat16)
    square = batched("sij,sjk->sik", scaled_low, scaled_low)
    square_low = lax.optimization_barrier(square.astype(jnp.bfloat16))
    mixed_low = (square_low.astype(jnp.float32) - 9.0 * scaled).astype(jnp.bfloat16)
    quartic = batched("sij,sjk->sik", square_low, mixed_low)
    identity = jnp.eye(statistic.shape[-1], dtype=jnp.float32)
    root_value = 36.0 * identity - 39.0 * scaled + 27.0 * square_low.astype(jnp.float32) + quartic
    return root_value.astype(jnp.bfloat16)


def precondition(grad_block, left_prev, right_prev, left_gram):
    left_stat = DECAY * left_prev.astype(jnp.float32) + (1.0 - DECAY) * left_gram
    right_stat = DECAY * right_prev.astype(jnp.float32) + (1.0 - DECAY) * batched(
        "sji,sjk->sik", grad_block, grad_block
    )
    left_root = inverse_root(left_stat)
    right_root = inverse_root(right_stat)
    half_done = batched("sij,sjk->sik", left_root, grad_block).astype(jnp.bfloat16)
    precond = batched("sij,sjk->sik", half_done, right_root)
    grad_wide = grad_block.astype(jnp.float32)
    grad_power = jnp.mean(grad_wide * grad_wide, axis=(1, 2), keepdims=True)
    cond_power = jnp.mean(precond * precond, axis=(1, 2), keepdims=True)
    graft_scale = jnp.sqrt(grad_power) / jnp.sqrt(cond_power + EPSILON)
    return (precond * graft_scale).astype(jnp.bfloat16)


def body(grad_part, owner_table, left_stats, right_stats):
    summed = lax.psum_scatter(grad_part[0], "dp", scatter_dimension=0, tiled=True).astype(
        jnp.float32
    )
    gradient = summed.astype(jnp.bfloat16)
    group_count = gradient.shape[0]
    row_count = gradient.shape[1]
    block_order = gradient.shape[2]
    owner_count = lax.axis_size("block")
    placing = (jnp.arange(owner_count, dtype=jnp.int32)[:, None] == owner_table[None, :]).astype(
        jnp.bfloat16
    )
    flattened = gradient.reshape(group_count, row_count * block_order)
    outgoing = jnp.dot(placing, flattened, preferred_element_type=jnp.float32).astype(jnp.bfloat16)
    outgoing = outgoing.reshape(owner_count, row_count, block_order)
    left_prev = left_stats[0, 0][None]
    right_prev = right_stats[0, 0][None]
    arrived = lax.all_to_all(outgoing, "block", split_axis=0, concat_axis=0, tiled=True)
    grad_block = arrived.reshape(1, block_order, block_order)
    left_gram = batched("sij,skj->sik", grad_block, grad_block)
    finished = precondition(grad_block, left_prev, right_prev, left_gram)
    returned = lax.all_to_all(
        finished.reshape(owner_count, row_count, block_order),
        "block",
        split_axis=0,
        concat_axis=0,
        tiled=True,
    )
    restored = lax.dot_general(
        placing,
        returned.reshape(owner_count, row_count * block_order),
        (((0,), (0,)), ((), ())),
        preferred_element_type=jnp.float32,
    )
    return restored.astype(jnp.bfloat16).reshape(group_count, row_count, block_order)


def solution(mesh):
    placed = (
        P("dp", None, "block", None),
        P("dp"),
        P("dp", "block", None, None),
        P("dp", "block", None, None),
    )
    return jax.shard_map(
        body, mesh=mesh, in_specs=placed, out_specs=P("dp", "block", None), check_vma=False
    )
```

profile of v0, /device:TPU:1, one launch (start us, length us, event | category | flops | bytes accessed | tf_op | source)
XLA Modules:
  0.0 152.0 jit_solution(1315372849539271715)
XLA Ops:
  6.5 0.7 reduce-scatter.2.cloned.1.call-update
  7.3 63.3 %reduce-scatter.2.cloned.1.call-done = bf16[16,8,512]{2,1,0:T(8,128)(2,1)} async-done(((bf16[192,8,512]{2,1,0:T(8,128)(2,1)}), bf16[16,8,512]{2,1,0:T(8,128)(2,1)}) %reduce-scatter.2.cloned.1.call-update) | async-done | bytes 131088 | tf_op jit(solution)/shard_map/reduce_scatter | solution.py:44
  70.6 0.9 copy.34
  71.5 0.3 convolution_convert_fusion
  71.8 1.0 copy.35
  72.8 17.7 %all-to-all-start = ((bf16[64,8,512]{2,1,0:T(8,128)(2,1)}), bf16[64,8,512]{2,1,0:T(8,128)(2,1)S(1)}, u32[]{:S(2)}, u32[]{:S(2)}) async-start(bf16[64,8,512]{2,1,0:T(8,128)(2,1)} %bitcast.23), calls=%async_computation.1 | async-start | bytes 1048576 | tf_op jit(solution)/shard_map/all_to_all | solution.py:60
  90.5 0.2 copy.20
  90.7 0.2 copy.23
  90.9 17.3 %all-to-all-done = bf16[64,8,512]{2,1,0:T(8,128)(2,1)S(1)} async-done(((bf16[64,8,512]{2,1,0:T(8,128)(2,1)}), bf16[64,8,512]{2,1,0:T(8,128)(2,1)S(1)}, u32[]{:S(2)}, u32[]{:S(2)}) %all-to-all-start) | async-done | bytes 524320 | tf_op jit(solution)/shard_map/all_to_all | solution.py:60
  108.2 0.5 abs_reduce_fusion.1
  108.7 0.6 reduce_max.18
  109.3 1.1 fusion.10
  110.4 1.2 fusion.7
  111.6 0.6 abs_reduce_fusion
  112.2 0.6 reduce_max.19
  112.8 1.1 fusion.11
  113.9 2.0 %fusion.8 = bf16[512,512]{0,1:T(8,128)(2,1)} fusion(bf16[1,512,512]{1,2,0:T(8,128)(2,1)S(1)} %fusion.11, f32[512,512]{0,1:T(8,128)S(1)} %get-tuple-element.6, f32[]{:T(128)} %reduce_max.19), kind=kOutput, calls=%fused_computation.23 | convolution fusion | flops 272367616 | bytes 2097156 | tf_op jit(solution)/shard_map/sij,sjk->sik/dot_general | solution.py:11
  115.9 2.5 %multiply_reduce_fusion = (f32[]{:T(128)}, f32[512,512]{1,0:T(8,128)S(1)}) fusion(bf16[512,512]{0,1:T(8,128)(2,1)} %fusion.8, bf16[512,512]{0,1:T(8,128)(2,1)S(1)} %fusion.7, bf16[64,8,512]{2,1,0:T(8,128)(2,1)S(1)} %all-to-all-done), kind=kOutput, calls=%fused_computation.34 | convolution fusion | flops 537657344 | bytes 2621444 | tf_op jit(solution)/shard_map/sij,sjk->sik/dot_general | solution.py:11
  119.1 0.9 multiply_reduce_fusion.1
  120.6 0.1 fusion.18
  120.8 23.2 %all_to_all.10 = bf16[64,8,512]{2,1,0:T(8,128)(2,1)S(1)} all-to-all(bf16[64,8,512]{2,1,0:T(8,128)(2,1)S(1)} %fusion.18), channel_id=1, replica_groups=mesh['dp'=12,'block'=64] {'block'}, dimensions={0} | all-to-all | bytes 1048576 | tf_op jit(solution)/shard_map/all_to_all | solution.py:64
  144.0 0.2 copy.36
  144.2 0.2 convolution_convert_fusion.1
  144.4 0.7 copy.37
  (7 shorter events, 0.0 us)
Async XLA Ops:
  6.5 65.0 %copy-start.2 = (s32[16]{0:T(128)S(1)}, s32[16]{0:T(128)}, u32[]{:S(2)}) copy-start(s32[16]{0:T(128)} %param.5) | copy-start | bytes 196
  6.5 64.0 %reduce-scatter.2.cloned.1.call-start = ((), (), s32[]{:S(2)}) async-start(), calls=%async_computation.3 | async-start | bytes 1703936 | tf_op jit(solution)/shard_map/reduce_scatter | solution.py:44
  7.3 83.2 %copy-start = (bf16[1,1,512,512]{3,2,1,0:T(8,128)(2,1)S(1)}, bf16[1,1,512,512]{3,2,1,0:T(8,128)(2,1)}, u32[]{:S(2)}) copy-start(bf16[1,1,512,512]{3,2,1,0:T(8,128)(2,1)} %param.6) | copy-start | bytes 1572868
  71.8 18.9 %copy-start.1 = (bf16[1,1,512,512]{3,2,1,0:T(8,128)(2,1)S(1)}, bf16[1,1,512,512]{3,2,1,0:T(8,128)(2,1)}, u32[]{:S(2)}) copy-start(bf16[1,1,512,512]{3,2,1,0:T(8,128)(2,1)} %param.7) | copy-start | bytes 1572868
  72.8 35.4 %all-to-all-start = ((bf16[64,8,512]{2,1,0:T(8,128)(2,1)}), bf16[64,8,512]{2,1,0:T(8,128)(2,1)S(1)}, u32[]{:S(2)}, u32[]{:S(2)}) async-start(bf16[64,8,512]{2,1,0:T(8,128)(2,1)} %bitcast.23), calls=%async_computation.1 | async-start | bytes 1048576 | tf_op jit(solution)/shard_map/all_to_all | solution.py:60
Sparse Core Ops, SparseCore 0:
  10.5 60.0 reduce-scatter.1
where the time goes:
time: 152 us
  waiting for transfers between devices  81.3 us (53%)
  blocking collectives  23.2 us (15%)
  starting transfers between devices  17.7 us (12%)
  between operations  14.9 us (10%)
  matrix products  9.45 us (6%)
  local copies, waits for them, and re-layouts  3.23 us (2%)
  other arithmetic  2.2 us (1%)
    reduce_scatter x1, waiting for transfers between devices, body(): lax.psum_scatter(grad_part[0], 'dp', scatter_dimension=0, tiled=True)  63.3 us
    all_to_all x1, blocking collectives, body(): lax.all_to_all(finished.reshape(owner_count, row_count, block_order), 'bl...  23.2 us
    all_to_all x1, starting transfers between devices, body(): lax.all_to_all(outgoing, 'block', split_axis=0, concat_axis=0, tiled=True)  17.7 us
    all_to_all x1, waiting for transfers between devices, body(): lax.all_to_all(outgoing, 'block', split_axis=0, concat_axis=0, tiled=True)  17.3 us
    dot_general x7, matrix products, batched(): jnp.einsum(pattern, left_side, right_side, preferred_element_type=jnp.flo...  8.95 us
    unnamed x12, local copies, waits for them, and re-layouts  3.23 us
  transfers between devices with their start and end apart: 2, of which 2 were waited for; matrix products, arithmetic and copies ran while one was open for 0% of the time, Pallas kernels for 0%

commit v1 on v0

v1 whole, which is shorter than its diff:
```python
import functools

import jax
import jax.numpy as jnp
from jax import lax
from jax.experimental import pallas as pl
from jax.experimental.pallas import tpu as pltpu
from jax.sharding import PartitionSpec as P

DECAY = 0.9
EPSILON = 1e-06
MESH = pl.DeviceIdType.MESH
F32 = jnp.float32
BF16 = jnp.bfloat16


def site_of(j):
    return 4 * j + 2 * lax.rem(j // 2, 2)


def wide_dot(a, b, contract):
    return lax.dot_general(a, b, ((contract[0], contract[1]), ((), ())), preferred_element_type=F32)


def kernel(nz, nb, grp, table, gp, left, right, out,
           zrecv, zstage, gbuf, statbuf, selbuf, statfull, g_ref, gt_ref,
           wide_l, wide_r, low_l, low_r, sq_l, sq_r, mix_l, mix_r, upd, rbuf,
           z_send, z_recv, g_send, g_recv, s_send, s_recv, f_send, f_recv, u_send, u_recv, local_sem):
    z = lax.axis_index("dp")
    me = lax.axis_index("block")
    order = 8 * nb
    cw = order // 4
    rows = grp * 8
    half = nz // 2
    own_site = me // 4
    is_site = me == site_of(own_site)

    def there(dp, block):
        return {"dp": dp, "block": block}

    barrier = pltpu.get_barrier_semaphore()
    up, down = lax.rem(z + 1, nz), lax.rem(z + nz - 1, nz)
    for neighbour in (up, down):
        pl.semaphore_signal(barrier, inc=1, device_id=there(neighbour, me), device_id_type=MESH)

    @pl.loop(1, nb)
    def _(r):
        pl.semaphore_signal(barrier, inc=1, device_id=there(z, lax.rem(me + r, nb)), device_id_type=MESH)

    pl.semaphore_wait(barrier, nb + 1)

    def column(k):
        return pl.ds(k * cw, cw)

    def own_rows(d):
        return pl.ds(pl.multiple_of(d * rows, rows), rows)

    def arc(k, way):
        return half if (k + way) % 2 == 0 else half - 1

    def hop(src, way, k, s):
        return pltpu.make_async_remote_copy(
            src_ref=src, dst_ref=zrecv.at[way, k, s],
            send_sem=z_send.at[way, k, s], recv_sem=z_recv.at[way, k, s],
            device_id=there(up if way == 0 else down, me), device_id_type=MESH)

    def target(way, dist):
        return lax.rem(z + dist, nz) if way == 0 else lax.rem(z + nz - dist, nz)

    def begin(s):
        for k in range(4):
            for way in range(2):
                if half - arc(k, way) == s:
                    d = target(way, half - s)
                    hop(gp.at[own_rows(d), column(k)], way, k, s).start()

    def onward(s, k, way):
        held = zrecv.at[way, k, s - 1]
        hop(held, way, k, s - 1).wait_recv()
        d = target(way, half - s)
        held[...] = (held[...].astype(F32) + gp[own_rows(d), column(k)].astype(F32)).astype(BF16)
        hop(held, way, k, s).start()

    begin(0)
    begin(1)

    def stat_copy(source, first, d, who):
        return pltpu.make_async_remote_copy(
            src_ref=source.at[pl.ds(pl.multiple_of(first, 16), 16)], dst_ref=statbuf.at[me],
            send_sem=s_send, recv_sem=s_recv, device_id=there(z, who), device_id_type=MESH)

    hb = nb // 2

    @pl.loop(1, nb)
    def _(r):
        d = lax.rem(me + r, nb)

        @pl.when(d < hb)
        def _():
            stat_copy(left, 16 * d, d, d).start()

        @pl.when(d >= hb)
        def _():
            stat_copy(right, 16 * (d - hb), d, d).start()

    @pl.when(me < hb)
    def _():
        c = pltpu.make_async_copy(left.at[pl.ds(pl.multiple_of(16 * me, 16), 16)], statbuf.at[me], local_sem)
        c.start()
        c.wait()

    @pl.when(me >= hb)
    def _():
        c = pltpu.make_async_copy(right.at[pl.ds(pl.multiple_of(16 * (me - hb), 16), 16)], statbuf.at[me], local_sem)
        c.start()
        c.wait()

    for k in range(4):
        for way in range(2):
            if arc(k, way) == half:
                onward(1, k, way)

    @pl.loop(2, half)
    def _(s):
        for k in range(4):
            for way in range(2):
                onward(s, k, way)

    for w in range(2):
        parts = []
        for k in (2 * w, 2 * w + 1):
            for way in range(2):
                hop(zrecv.at[way, k, half - 1], way, k, half - 1).wait_recv()
            total = (gp[own_rows(z), column(k)].astype(F32) + zrecv[0, k, half - 1].astype(F32)
                     + zrecv[1, k, half - 1].astype(F32))
            parts.append(total.reshape(grp, 8, cw))
        zstage[w] = jnp.concatenate(parts, axis=1).astype(BF16)

        @pl.loop(0, grp)
        def _(i):
            j = lax.rem(own_site + i, grp)
            who = site_of(j)

            @pl.when(who != me)
            def _():
                pltpu.make_async_remote_copy(
                    src_ref=zstage.at[w, j], dst_ref=gbuf.at[w, me],
                    send_sem=g_send.at[w], recv_sem=g_recv.at[w],
                    device_id=there(z, who), device_id_type=MESH).start()

        @pl.when(is_site)
        def _():
            gbuf[w, me] = zstage[w, own_site]

    def settle(ref, sem):
        pltpu.make_async_copy(ref, ref, sem).wait()

    settle(statbuf.at[pl.ds(0, nb - 1)], s_recv)

    @pl.loop(0, grp)
    def _(i):
        j = lax.rem(own_site + i, grp)
        selbuf[j] = statbuf[table[j]]
        who = site_of(j)

        @pl.when(who != me)
        def _():
            pltpu.make_async_remote_copy(
                src_ref=selbuf.at[j], dst_ref=statfull.at[me],
                send_sem=f_send, recv_sem=f_recv,
                device_id=there(z, who), device_id_type=MESH).start()

    @pl.when(is_site)
    def _():
        statfull[me] = selbuf[own_site]

    @pl.when(is_site)
    def _():
        for w in range(2):
            settle(gbuf.at[w, pl.ds(0, nb - 1)], g_recv.at[w])
            pieces = gbuf[w].astype(F32).reshape(nb, 2, 8, cw)
            for h in range(2):
                piece = pieces[:, h].reshape(order, cw).astype(BF16)
                g_ref[:, column(2 * w + h)] = piece
                gt_ref[column(2 * w + h), :] = piece.T
        settle(statfull.at[pl.ds(0, nb - 1)], f_recv)
        nr = 2
        rb = order // nr
        blocks = [pl.ds(i * rb, rb) for i in range(nr)]
        sides = ((0, g_ref, gt_ref, wide_l, low_l, sq_l, mix_l), (hb, gt_ref, g_ref, wide_r, low_r, sq_r, mix_r))
        bounds = []
        for first, a, b, wide, low, sq, mix in sides:
            sums = jnp.zeros((1, order), F32)
            for i, rs in enumerate(blocks):
                prev = statfull[pl.ds(first + i * (rb // 16), rb // 16)].reshape(rb, order).astype(F32)
                stat = DECAY * prev + (1.0 - DECAY) * wide_dot(a[rs, :], b[...], ((1,), (0,)))
                wide[rs, :] = stat
                sums = sums + jnp.sum(jnp.abs(stat), axis=0, keepdims=True)
            bounds.append(jnp.max(sums, axis=1, keepdims=True))
        for (first, a, b, wide, low, sq, mix), bound in zip(sides, bounds):
            scale = 1.0 / bound
            for rs in blocks:
                scaled = wide[rs, :] * scale
                wide[rs, :] = scaled
                low[rs, :] = scaled.astype(BF16)
        for first, a, b, wide, low, sq, mix in sides:
            for rs in blocks:
                square = wide_dot(low[rs, :], low[...], ((1,), (0,))).astype(BF16)
                sq[rs, :] = square
                mix[rs, :] = (square.astype(F32) - 9.0 * wide[rs, :]).astype(BF16)
        for first, a, b, wide, low, sq, mix in sides:
            for i, rs in enumerate(blocks):
                eye = (lax.broadcasted_iota(jnp.int32, (rb, order), 0) + i * rb
                       == lax.broadcasted_iota(jnp.int32, (rb, order), 1)).astype(F32)
                square = sq[rs, :]
                quartic = wide_dot(square, mix[...], ((1,), (0,)))
                low[rs, :] = (36.0 * eye - 39.0 * wide[rs, :] + 27.0 * square.astype(F32) + quartic).astype(BF16)
        grad_sum = jnp.zeros((1, order), F32)
        cond_sum = jnp.zeros((1, order), F32)
        for rs in blocks:
            done = wide_dot(low_l[rs, :], g_ref[...], ((1,), (0,))).astype(BF16)
            cond = wide_dot(done, low_r[...], ((1,), (0,)))
            wide_l[rs, :] = cond
            grad = g_ref[rs, :].astype(F32)
            grad_sum = grad_sum + jnp.sum(grad * grad, axis=0, keepdims=True)
            cond_sum = cond_sum + jnp.sum(cond * cond, axis=0, keepdims=True)
        count = 1.0 / (order * order)
        grad_power = jnp.sum(grad_sum, axis=1, keepdims=True) * count
        cond_power = jnp.sum(cond_sum, axis=1, keepdims=True) * count
        graft = jnp.sqrt(grad_power) / jnp.sqrt(cond_power + EPSILON)
        for i, rs in enumerate(blocks):
            update = wide_l[rs, :] * graft
            halves = [update[:, h * 2 * cw:(h + 1) * 2 * cw].reshape(rb // 8, 8, 2 * cw) for h in range(2)]
            upd[pl.ds(i * (rb // 8), rb // 8)] = jnp.concatenate(halves, axis=1).astype(BF16)

        @pl.loop(1, nb)
        def _(r):
            d = lax.rem(me + r, nb)
            pltpu.make_async_remote_copy(
                src_ref=upd.at[d], dst_ref=rbuf.at[own_site],
                send_sem=u_send, recv_sem=u_recv,
                device_id=there(z, d), device_id_type=MESH).start()

        rbuf[own_site] = upd[me]
        settle(rbuf.at[pl.ds(0, grp - 1)], u_recv)
        settle(upd.at[pl.ds(0, nb - 1)], u_send)

    @pl.when(jnp.logical_not(is_site))
    def _():
        settle(rbuf, u_recv)

    returned = rbuf[...].astype(F32).reshape(grp, 2, 8, 2 * cw)
    for h in range(2):
        out[:, h * 2 * cw:(h + 1) * 2 * cw] = returned[:, h].reshape(rows, 2 * cw).astype(BF16)

    settle(statbuf.at[pl.ds(0, nb - 1)], s_send)

    @pl.when(is_site)
    def _():
        settle(selbuf.at[pl.ds(0, grp - 1)], f_send)
        for w in range(2):
            settle(zstage.at[w, pl.ds(0, grp - 1)], g_send.at[w])

    @pl.when(jnp.logical_not(is_site))
    def _():
        settle(selbuf, f_send)
        for w in range(2):
            settle(zstage.at[w], g_send.at[w])

    for k in range(4):
        for way in range(2):
            first = half - arc(k, way)

            @pl.loop(first, half)
            def _(s):
                hop(zrecv.at[way, k, s], way, k, s).wait_send()


def body(grad_part, owner_table, left_stats, right_stats):
    nz, nb = lax.axis_size("dp"), lax.axis_size("block")
    grp = owner_table.shape[0]
    order = left_stats.shape[-1]
    cw, rows, half = order // 4, grp * 8, nz // 2
    vmem, dma = pltpu.VMEM, pltpu.SemaphoreType.DMA
    out = pl.pallas_call(
        functools.partial(kernel, nz, nb, grp),
        out_shape=jax.ShapeDtypeStruct((rows, order), BF16),
        in_specs=[pl.BlockSpec(memory_space=pltpu.SMEM), pl.BlockSpec(memory_space=pltpu.VMEM),
                  pl.BlockSpec(memory_space=pl.ANY), pl.BlockSpec(memory_space=pl.ANY)],
        out_specs=pl.BlockSpec(memory_space=pltpu.VMEM),
        scratch_shapes=[
            vmem((2, 4, half, rows, cw), BF16), vmem((2, grp, 16, cw), BF16), vmem((2, nb, 16, cw), BF16),
            vmem((nb, 16, order), BF16), vmem((grp, 16, order), BF16), vmem((nb, 16, order), BF16),
            vmem((order, order), BF16), vmem((order, order), BF16),
            vmem((order, order), F32), vmem((order, order), F32),
            vmem((order, order), BF16), vmem((order, order), BF16), vmem((order, order), BF16),
            vmem((order, order), BF16), vmem((order, order), BF16), vmem((order, order), BF16),
            vmem((nb, 16, 2 * cw), BF16), vmem((grp, 16, 2 * cw), BF16),
            dma((2, 4, half)), dma((2, 4, half)), dma((2,)), dma((2,)),
            dma, dma, dma, dma, dma, dma, dma,
        ],
        compiler_params=pltpu.CompilerParams(
            collective_id=0, has_side_effects=True, vmem_limit_bytes=40 * 1024 * 1024),
    )(owner_table, grad_part.reshape(nz * rows, order), left_stats[0, 0], right_stats[0, 0])
    return out.reshape(grp, 8, order)


def solution(mesh):
    placed = (
        P("dp", None, "block", None),
        P("dp"),
        P("dp", "block", None, None),
        P("dp", "block", None, None),
    )
    return jax.shard_map(
        body, mesh=mesh, in_specs=placed, out_specs=P("dp", "block", None), check_vma=False
    )
```

time: 152 us -> 74.3 us (0.49)
  waiting for transfers between devices: 81.3 us -> 0 us
  Pallas kernels: 0 us -> 69.2 us
  blocking collectives: 23.2 us -> 0 us
  starting transfers between devices: 17.7 us -> 0 us
  between operations: 14.9 us -> 0.01 us
  matrix products: 9.45 us -> 0 us
  other arithmetic: 2.2 us -> 0 us
  local copies, waits for them, and re-layouts: 3.23 us -> 4.8 us
    pallas_call x0 -> x1, Pallas kernels: none -> 69.2 us  [body(): pl.pallas_call(functools.partial(kernel, nz, nb, grp), out_shape=jax.Shap...]
    reduce_scatter x1 -> x0, waiting for transfers between devices: 63.3 us -> none  [body(): lax.psum_scatter(grad_part[0], 'dp', scatter_dimension=0, tiled=True)]
    all_to_all x1 -> x0, blocking collectives: 23.2 us -> none  [body(): lax.all_to_all(finished.reshape(owner_count, row_count, block_order), 'bl...]
    all_to_all x1 -> x0, starting transfers between devices: 17.7 us -> none  [body(): lax.all_to_all(outgoing, 'block', split_axis=0, concat_axis=0, tiled=True)]
    all_to_all x1 -> x0, waiting for transfers between devices: 17.3 us -> none  [body(): lax.all_to_all(outgoing, 'block', split_axis=0, concat_axis=0, tiled=True)]
    dot_general x9 -> x0, matrix products: 9.45 us -> none  [the longest x7 8.95 us: batched(): jnp.einsum(pattern, left_side, right_side, preferred_element_type=jnp.flo...]
    unnamed x12 -> x9, local copies, waits for them, and re-layouts: 3.23 us -> 4.8 us
  transfers between devices with their start and end apart: 2 -> 0, of which waited for: 2 -> 0; matrix products, arithmetic and copies ran while one was open for 0% -> 0% of each run, Pallas kernels for 0% -> 0%
where the time goes in v1:
time: 74.3 us; the launch traced here: 74 us
  Pallas kernels  69.2 us (93%)
  local copies, waits for them, and re-layouts  4.8 us (6%)
    pallas_call x1, Pallas kernels, body(): pl.pallas_call(functools.partial(kernel, nz, nb, grp), out_shape=jax.Shap...  69.2 us
    unnamed x9, local copies, waits for them, and re-layouts  4.8 us

profile of v1, /device:TPU:1, one launch (start us, length us, event | category | flops | bytes accessed | tf_op | source)
XLA Modules:
  0.0 74.0 jit_solution(30901093184669959)
XLA Ops:
  0.0 0.0 copy-start
  0.0 1.4 %copy-done = bf16[1,192,8,512]{3,2,1,0:T(8,128)(2,1)S(1)} copy-done((bf16[1,192,8,512]{3,2,1,0:T(8,128)(2,1)S(1)}, bf16[1,192,8,512]{3,2,1,0:T(8,128)(2,1)}, u32[]{:S(2)}) %copy-start) | copy-done | bytes 1572888
  1.4 0.0 copy-start.1
  1.4 1.0 %copy-done.1 = bf16[1,1,512,512]{3,2,1,0:T(8,128)(2,1)S(1)} copy-done((bf16[1,1,512,512]{3,2,1,0:T(8,128)(2,1)S(1)}, bf16[1,1,512,512]{3,2,1,0:T(8,128)(2,1)}, u32[]{:S(2)}) %copy-start.1) | copy-done | bytes 524312
  2.5 0.0 copy-start.2
  2.5 1.0 %copy-done.2 = bf16[1,1,512,512]{3,2,1,0:T(8,128)(2,1)S(1)} copy-done((bf16[1,1,512,512]{3,2,1,0:T(8,128)(2,1)S(1)}, bf16[1,1,512,512]{3,2,1,0:T(8,128)(2,1)}, u32[]{:S(2)}) %copy-start.2) | copy-done | bytes 524312
  3.5 0.0 copy-start.3
  3.5 0.7 copy-done.3
  4.1 69.2 %shard_map.46 = bf16[128,512]{1,0:T(8,128)(2,1)S(1)} custom-call(s32[16]{0:T(128)S(1)} %copy-done.3, bf16[1536,512]{1,0:T(8,128)(2,1)S(1)} %bitcast.4, bf16[512,512]{1,0:T(8,128)(2,1)S(1)} %bitcast.6, bf16[512,512]{1,0:T(8,128)(2,1)S(1)} %bitcast.7), custom_call_target="tpu_custom_call" | custom-call | tf_op jit(solution)/shard_map/pallas_call | solution.py:285
  73.3 0.7 copy.6
Async XLA Ops:
  0.0 1.4 %copy-start = (bf16[1,192,8,512]{3,2,1,0:T(8,128)(2,1)S(1)}, bf16[1,192,8,512]{3,2,1,0:T(8,128)(2,1)}, u32[]{:S(2)}) copy-start(bf16[1,192,8,512]{3,2,1,0:T(8,128)(2,1)} %param.4) | copy-start | bytes 4718596
  1.4 1.0 %copy-start.1 = (bf16[1,1,512,512]{3,2,1,0:T(8,128)(2,1)S(1)}, bf16[1,1,512,512]{3,2,1,0:T(8,128)(2,1)}, u32[]{:S(2)}) copy-start(bf16[1,1,512,512]{3,2,1,0:T(8,128)(2,1)} %param.6) | copy-start | bytes 1572868
  2.5 1.0 %copy-start.2 = (bf16[1,1,512,512]{3,2,1,0:T(8,128)(2,1)S(1)}, bf16[1,1,512,512]{3,2,1,0:T(8,128)(2,1)}, u32[]{:S(2)}) copy-start(bf16[1,1,512,512]{3,2,1,0:T(8,128)(2,1)} %param.7) | copy-start | bytes 1572868
  3.5 0.7 copy-start.3

commit v2 on v1

--- a/solution.py
+++ b/solution.py
@@ -15,17 +15,23 @@
 
 
 def site_of(j):
-    return 4 * j + 2 * lax.rem(j // 2, 2)
+    return 4 * j + 2 * lax.rem(j // 2, 2) + 1
+
+
+def zigzag(i, n):
+    return n // 2 + jnp.where(lax.rem(i, 2) == 1, -((i + 1) // 2), i // 2)
 
 
 def wide_dot(a, b, contract):
     return lax.dot_general(a, b, ((contract[0], contract[1]), ((), ())), preferred_element_type=F32)
 
 
-def kernel(nz, nb, grp, table, gp, left, right, out,
-           zrecv, zstage, gbuf, statbuf, selbuf, statfull, g_ref, gt_ref,
+def kernel(nz, nb, grp, table, gp_hbm, left, right, out, gp, gp_sem,
+           zrecv, zstage, gbuf, l_ref, r_ref, pair, statbuf, selbuf, statfull, m_ref, mt_ref,
+           diag, diags, g_ref, gt_ref,
            wide_l, wide_r, low_l, low_r, sq_l, sq_r, mix_l, mix_r, upd, rbuf,
-           z_send, z_recv, g_send, g_recv, s_send, s_recv, f_send, f_recv, u_send, u_recv, local_sem):
+           z_send, z_recv, g_send, g_recv, s_send, s_recv, f_send, f_recv, u_send, u_recv, d_send, d_recv,
+           l_sem, r_sem):
     z = lax.axis_index("dp")
     me = lax.axis_index("block")
     order = 8 * nb
@@ -38,16 +44,73 @@
     def there(dp, block):
         return {"dp": dp, "block": block}
 
+    up, down = lax.rem(z + 1, nz), lax.rem(z + nz - 1, nz)
+    hb = nb // 2
+    load = pltpu.make_async_copy(gp_hbm, gp, gp_sem)
+    load.start()
+    load_l = pltpu.make_async_copy(left, l_ref, l_sem)
+    load_l.start()
+    load_r = pltpu.make_async_copy(right, r_ref, r_sem)
+    load_r.start()
+
+    def each_peer(low, high, act):
+        if low == 0:
+            act(lax.rem(me + hb, nb))
+            low = 1
+
+        @pl.loop(low, high)
+        def _(i):
+            act(lax.rem(me + (hb + i), nb))
+            act(lax.rem(me + (hb - i), nb))
+
+    def peer_site(i):
+        return lax.rem(own_site + zigzag(i, grp), grp)
+
     barrier = pltpu.get_barrier_semaphore()
-    up, down = lax.rem(z + 1, nz), lax.rem(z + nz - 1, nz)
     for neighbour in (up, down):
         pl.semaphore_signal(barrier, inc=1, device_id=there(neighbour, me), device_id_type=MESH)
 
-    @pl.loop(1, nb)
-    def _(r):
-        pl.semaphore_signal(barrier, inc=1, device_id=there(z, lax.rem(me + r, nb)), device_id_type=MESH)
-
-    pl.semaphore_wait(barrier, nb + 1)
+    each_peer(0, hb, lambda d: pl.semaphore_signal(
+        barrier, inc=1, device_id=there(z, d), device_id_type=MESH))
+
+    load_l.wait()
+    load_r.wait()
+    rb4 = order // 4
+    for i in range(4):
+        rs = pl.ds(i * rb4, rb4)
+        row = lax.broadcasted_iota(jnp.int32, (rb4, order), 0) + i * rb4
+        col = lax.broadcasted_iota(jnp.int32, (rb4, order), 1)
+        right_rows = r_ref[rs, :].astype(F32)
+        both = jnp.where(col >= row, l_ref[rs, :].astype(F32), right_rows).astype(BF16)
+        for h in range(2):
+            pair[h, rs, :] = both[:, h * 2 * cw:(h + 1) * 2 * cw]
+        on_diagonal = jnp.sum(jnp.where(col == row, right_rows, 0.0), axis=0, keepdims=True)
+        diag[pl.ds(i, 1), :] = on_diagonal[:, i * cw:(i + 1) * cw]
+    diag[pl.ds(4, 4), :] = jnp.zeros((4, cw), F32)
+    statbuf[me] = pair[me // hb, pl.ds(pl.multiple_of(16 * lax.rem(me, hb), 16), 16), :]
+
+    @pl.when(is_site)
+    def _():
+        diags[me] = diag[...]
+
+    def spread(low, high):
+        def act(d):
+            pltpu.make_async_remote_copy(
+                src_ref=pair.at[d // hb, pl.ds(pl.multiple_of(16 * lax.rem(d, hb), 16), 16)], dst_ref=statbuf.at[me],
+                send_sem=s_send, recv_sem=s_recv, device_id=there(z, d), device_id_type=MESH).start()
+
+        each_peer(low, high, act)
+
+    def spread_diagonal():
+        @pl.loop(0, grp)
+        def _(i):
+            who = site_of(peer_site(i))
+
+            @pl.when(who != me)
+            def _():
+                pltpu.make_async_remote_copy(
+                    src_ref=diag, dst_ref=diags.at[me], send_sem=d_send, recv_sem=d_recv,
+                    device_id=there(z, who), device_id_type=MESH).start()
 
     def column(k):
         return pl.ds(k * cw, cw)
@@ -67,9 +130,9 @@
     def target(way, dist):
         return lax.rem(z + dist, nz) if way == 0 else lax.rem(z + nz - dist, nz)
 
-    def begin(s):
+    def begin(s, ways):
         for k in range(4):
-            for way in range(2):
+            for way in ways:
                 if half - arc(k, way) == s:
                     d = target(way, half - s)
                     hop(gp.at[own_rows(d), column(k)], way, k, s).start()
@@ -81,50 +144,35 @@
         held[...] = (held[...].astype(F32) + gp[own_rows(d), column(k)].astype(F32)).astype(BF16)
         hop(held, way, k, s).start()
 
-    begin(0)
-    begin(1)
-
-    def stat_copy(source, first, d, who):
-        return pltpu.make_async_remote_copy(
-            src_ref=source.at[pl.ds(pl.multiple_of(first, 16), 16)], dst_ref=statbuf.at[me],
-            send_sem=s_send, recv_sem=s_recv, device_id=there(z, who), device_id_type=MESH)
-
-    hb = nb // 2
-
-    @pl.loop(1, nb)
-    def _(r):
-        d = lax.rem(me + r, nb)
-
-        @pl.when(d < hb)
-        def _():
-            stat_copy(left, 16 * d, d, d).start()
-
-        @pl.when(d >= hb)
-        def _():
-            stat_copy(right, 16 * (d - hb), d, d).start()
-
-    @pl.when(me < hb)
-    def _():
-        c = pltpu.make_async_copy(left.at[pl.ds(pl.multiple_of(16 * me, 16), 16)], statbuf.at[me], local_sem)
-        c.start()
-        c.wait()
-
-    @pl.when(me >= hb)
-    def _():
-        c = pltpu.make_async_copy(right.at[pl.ds(pl.multiple_of(16 * (me - hb), 16), 16)], statbuf.at[me], local_sem)
-        c.start()
-        c.wait()
+    load.wait()
+    third = hb // 3
+
+    pl.semaphore_wait(barrier, nb + 1)
+    begin(0, (0, 1))
+    begin(1, (0, 1))
+    spread(0, third)
 
     for k in range(4):
         for way in range(2):
             if arc(k, way) == half:
                 onward(1, k, way)
 
-    @pl.loop(2, half)
-    def _(s):
+    spread(third, 2 * third)
+
+    def all_onward(s):
         for k in range(4):
             for way in range(2):
                 onward(s, k, way)
+
+    if half > 2:
+        all_onward(2)
+
+    spread(2 * third, hb)
+    spread_diagonal()
+
+    @pl.loop(3, half)
+    def _(s):
+        all_onward(s)
 
     for w in range(2):
         parts = []
@@ -138,7 +186,7 @@
 
         @pl.loop(0, grp)
         def _(i):
-            j = lax.rem(own_site + i, grp)
+            j = peer_site(i)
             who = site_of(j)
 
             @pl.when(who != me)
@@ -159,7 +207,7 @@
 
     @pl.loop(0, grp)
     def _(i):
-        j = lax.rem(own_site + i, grp)
+        j = peer_site(i)
         selbuf[j] = statbuf[table[j]]
         who = site_of(j)
 
@@ -183,32 +231,44 @@
                 piece = pieces[:, h].reshape(order, cw).astype(BF16)
                 g_ref[:, column(2 * w + h)] = piece
                 gt_ref[column(2 * w + h), :] = piece.T
+        settle(diags.at[pl.ds(0, nb - 1)], d_recv)
+        chosen = diags[table[own_site]]
+        right_diag = jnp.concatenate([chosen[i:i + 1, :] for i in range(4)], axis=1)
         settle(statfull.at[pl.ds(0, nb - 1)], f_recv)
+        for h in range(2):
+            columns = statfull[pl.ds(h * hb, hb)].reshape(order, 2 * cw)
+            m_ref[:, h * 2 * cw:(h + 1) * 2 * cw] = columns
+            mt_ref[h * 2 * cw:(h + 1) * 2 * cw, :] = columns.T
         nr = 2
         rb = order // nr
         blocks = [pl.ds(i * rb, rb) for i in range(nr)]
-        sides = ((0, g_ref, gt_ref, wide_l, low_l, sq_l, mix_l), (hb, gt_ref, g_ref, wide_r, low_r, sq_r, mix_r))
+        sides = ((0, g_ref, gt_ref, wide_l, low_l, sq_l, mix_l), (1, gt_ref, g_ref, wide_r, low_r, sq_r, mix_r))
         bounds = []
-        for first, a, b, wide, low, sq, mix in sides:
+        for side, a, b, wide, low, sq, mix in sides:
             sums = jnp.zeros((1, order), F32)
             for i, rs in enumerate(blocks):
-                prev = statfull[pl.ds(first + i * (rb // 16), rb // 16)].reshape(rb, order).astype(F32)
+                row = lax.broadcasted_iota(jnp.int32, (rb, order), 0) + i * rb
+                col = lax.broadcasted_iota(jnp.int32, (rb, order), 1)
+                above, below = (m_ref, mt_ref) if side == 0 else (mt_ref, m_ref)
+                prev = jnp.where(col >= row, above[rs, :].astype(F32), below[rs, :].astype(F32))
+                if side == 1:
+                    prev = jnp.where(col == row, right_diag, prev)
                 stat = DECAY * prev + (1.0 - DECAY) * wide_dot(a[rs, :], b[...], ((1,), (0,)))
                 wide[rs, :] = stat
                 sums = sums + jnp.sum(jnp.abs(stat), axis=0, keepdims=True)
             bounds.append(jnp.max(sums, axis=1, keepdims=True))
-        for (first, a, b, wide, low, sq, mix), bound in zip(sides, bounds):
+        for (side, a, b, wide, low, sq, mix), bound in zip(sides, bounds):
             scale = 1.0 / bound
             for rs in blocks:
                 scaled = wide[rs, :] * scale
                 wide[rs, :] = scaled
                 low[rs, :] = scaled.astype(BF16)
-        for first, a, b, wide, low, sq, mix in sides:
+        for side, a, b, wide, low, sq, mix in sides:
             for rs in blocks:
                 square = wide_dot(low[rs, :], low[...], ((1,), (0,))).astype(BF16)
                 sq[rs, :] = square
                 mix[rs, :] = (square.astype(F32) - 9.0 * wide[rs, :]).astype(BF16)
-        for first, a, b, wide, low, sq, mix in sides:
+        for side, a, b, wide, low, sq, mix in sides:
             for i, rs in enumerate(blocks):
                 eye = (lax.broadcasted_iota(jnp.int32, (rb, order), 0) + i * rb
                        == lax.broadcasted_iota(jnp.int32, (rb, order), 1)).astype(F32)
@@ -233,14 +293,13 @@
             halves = [update[:, h * 2 * cw:(h + 1) * 2 * cw].reshape(rb // 8, 8, 2 * cw) for h in range(2)]
             upd[pl.ds(i * (rb // 8), rb // 8)] = jnp.concatenate(halves, axis=1).astype(BF16)
 
-        @pl.loop(1, nb)
-        def _(r):
-            d = lax.rem(me + r, nb)
+        def send_back(d):
             pltpu.make_async_remote_copy(
                 src_ref=upd.at[d], dst_ref=rbuf.at[own_site],
                 send_sem=u_send, recv_sem=u_recv,
                 device_id=there(z, d), device_id_type=MESH).start()
 
+        each_peer(0, hb, send_back)
         rbuf[own_site] = upd[me]
         settle(rbuf.at[pl.ds(0, grp - 1)], u_recv)
         settle(upd.at[pl.ds(0, nb - 1)], u_send)
@@ -258,12 +317,14 @@
     @pl.when(is_site)
     def _():
         settle(selbuf.at[pl.ds(0, grp - 1)], f_send)
+        settle(diags.at[pl.ds(0, grp - 1)], d_send)
         for w in range(2):
             settle(zstage.at[w, pl.ds(0, grp - 1)], g_send.at[w])
 
     @pl.when(jnp.logical_not(is_site))
     def _():
         settle(selbuf, f_send)
+        settle(diags.at[pl.ds(0, grp)], d_send)
         for w in range(2):
             settle(zstage.at[w], g_send.at[w])
 
@@ -285,22 +346,25 @@
     out = pl.pallas_call(
         functools.partial(kernel, nz, nb, grp),
         out_shape=jax.ShapeDtypeStruct((rows, order), BF16),
-        in_specs=[pl.BlockSpec(memory_space=pltpu.SMEM), pl.BlockSpec(memory_space=pltpu.VMEM),
-                  pl.BlockSpec(memory_space=pl.ANY), pl.BlockSpec(memory_space=pl.ANY)],
+        in_specs=[pl.BlockSpec(memory_space=pltpu.SMEM), pl.BlockSpec(memory_space=pltpu.HBM),
+                  pl.BlockSpec(memory_space=pltpu.HBM), pl.BlockSpec(memory_space=pltpu.HBM)],
         out_specs=pl.BlockSpec(memory_space=pltpu.VMEM),
-        scratch_shapes=[
+        scratch_shapes=[vmem((nz * rows, order), BF16), dma,
             vmem((2, 4, half, rows, cw), BF16), vmem((2, grp, 16, cw), BF16), vmem((2, nb, 16, cw), BF16),
-            vmem((nb, 16, order), BF16), vmem((grp, 16, order), BF16), vmem((nb, 16, order), BF16),
+            vmem((order, order), BF16), vmem((order, order), BF16), vmem((2, order, 2 * cw), BF16),
+            vmem((nb, 16, 2 * cw), BF16), vmem((grp, 16, 2 * cw), BF16), vmem((nb, 16, 2 * cw), BF16),
+            vmem((order, order), BF16), vmem((order, order), BF16),
+            vmem((8, cw), F32), vmem((nb, 8, cw), F32),
             vmem((order, order), BF16), vmem((order, order), BF16),
             vmem((order, order), F32), vmem((order, order), F32),
             vmem((order, order), BF16), vmem((order, order), BF16), vmem((order, order), BF16),
             vmem((order, order), BF16), vmem((order, order), BF16), vmem((order, order), BF16),
             vmem((nb, 16, 2 * cw), BF16), vmem((grp, 16, 2 * cw), BF16),
             dma((2, 4, half)), dma((2, 4, half)), dma((2,)), dma((2,)),
-            dma, dma, dma, dma, dma, dma, dma,
+            dma, dma, dma, dma, dma, dma, dma, dma, dma, dma,
         ],
         compiler_params=pltpu.CompilerParams(
-            collective_id=0, has_side_effects=True, vmem_limit_bytes=40 * 1024 * 1024),
+            collective_id=0, has_side_effects=True, vmem_limit_bytes=62 * 1024 * 1024),
     )(owner_table, grad_part.reshape(nz * rows, order), left_stats[0, 0], right_stats[0, 0])
     return out.reshape(grp, 8, order)
 

time: 74.3 us -> 64.4 us (0.87)
  Pallas kernels: 69.2 us -> 62.6 us
  local copies, waits for them, and re-layouts: 4.8 us -> 1.57 us
    pallas_call x1, Pallas kernels: 69.2 us -> 62.6 us  [body(): pl.pallas_call(functools.partial(kernel, nz, nb, grp), out_shape=jax.Shap...]
    unnamed x9 -> x1, local copies, waits for them, and re-layouts: 4.8 us -> 1.57 us
where the time goes in v2:
time: 64.4 us; the launch traced here: 64.2 us
  Pallas kernels  62.6 us (97%)
  local copies, waits for them, and re-layouts  1.57 us (2%)
    pallas_call x1, Pallas kernels, body(): pl.pallas_call(functools.partial(kernel, nz, nb, grp), out_shape=jax.Shap...  62.6 us
    unnamed x1, local copies, waits for them, and re-layouts  1.57 us

profile of v2, /device:TPU:1, one launch (start us, length us, event | category | flops | bytes accessed | tf_op | source)
XLA Modules:
  0.0 64.2 jit_solution(1067194317445660395)
XLA Ops:
  0.0 62.6 %shard_map.46 = bf16[128,512]{1,0:T(8,128)(2,1)} custom-call(s32[16]{0:T(128)} %table.1, bf16[1536,512]{1,0:T(8,128)(2,1)} %bitcast.4, bf16[512,512]{1,0:T(8,128)(2,1)} %bitcast.6, bf16[512,512]{1,0:T(8,128)(2,1)} %bitcast.7), custom_call_target="tpu_custom_call" | custom-call | tf_op jit(solution)/shard_map/pallas_call | solution.py:346
  62.6 1.6 %copy.6 = bf16[16,8,512]{2,1,0:T(8,128)(2,1)} copy(bf16[16,8,512]{2,1,0:T(8,128)(2,1)} %bitcast.5) | data formatting | bytes 262144

commit v3 on v2

--- a/solution.py
+++ b/solution.py
@@ -31,7 +31,7 @@
            diag, diags, g_ref, gt_ref,
            wide_l, wide_r, low_l, low_r, sq_l, sq_r, mix_l, mix_r, upd, rbuf,
            z_send, z_recv, g_send, g_recv, s_send, s_recv, f_send, f_recv, u_send, u_recv, d_send, d_recv,
-           l_sem, r_sem):
+           l_sem, r_sem, ready, token):
     z = lax.axis_index("dp")
     me = lax.axis_index("block")
     order = 8 * nb
@@ -66,12 +66,50 @@
     def peer_site(i):
         return lax.rem(own_site + zigzag(i, grp), grp)
 
+    cores, width = 2, 4
+    height = nb // (cores * width)
+    y, x, c = me // (cores * width), lax.rem(me // cores, width), lax.rem(me, cores)
+
+    def moved(dy, dx, dc):
+        return (lax.rem(y + dy + height, height) * width + lax.rem(x + dx + width, width)) * cores + lax.rem(c + dc, cores)
+
+    first_plane = z == 0
+    late = z >= half
     barrier = pltpu.get_barrier_semaphore()
+
+    def tell(semaphore, dp, block):
+        pl.semaphore_signal(semaphore, inc=1, device_id=there(dp, block), device_id_type=MESH)
+
     for neighbour in (up, down):
-        pl.semaphore_signal(barrier, inc=1, device_id=there(neighbour, me), device_id_type=MESH)
-
-    each_peer(0, hb, lambda d: pl.semaphore_signal(
-        barrier, inc=1, device_id=there(z, d), device_id_type=MESH))
+        @pl.when(neighbour != 0)
+        def _():
+            tell(barrier, neighbour, me)
+
+    @pl.when(late)
+    def _():
+        for dy, dx, dc in ((1, 0, 0), (-1, 0, 0), (0, 1, 0), (0, -1, 0), (0, 0, 1)):
+            tell(barrier, z, moved(dy, dx, dc))
+
+    @pl.when(jnp.logical_not(late))
+    def _():
+        each_peer(0, hb, lambda d: tell(barrier, z, d))
+
+    rounds = [((1, 0, 0), (-1, 0, 0), (0, 0, 1)),
+              ((2, 0, 0), (-2, 0, 0)) if height > 4 else (),
+              ((0, 1, 0), (0, -1, 0), (0, 1, 1), (0, -1, 1), (0, 0, 1)),
+              ((0, 2, 0), (0, 2, 1))]
+
+    def give(r):
+        @pl.when(late)
+        def _():
+            for step in rounds[r]:
+                tell(token.at[r], z, moved(*step))
+
+    def take(r):
+        @pl.when(late)
+        def _():
+            if rounds[r]:
+                pl.semaphore_wait(token.at[r], len(rounds[r]))
 
     load_l.wait()
     load_r.wait()
@@ -112,11 +150,10 @@
                     src_ref=diag, dst_ref=diags.at[me], send_sem=d_send, recv_sem=d_recv,
                     device_id=there(z, who), device_id_type=MESH).start()
 
-    def column(k):
-        return pl.ds(k * cw, cw)
-
-    def own_rows(d):
-        return pl.ds(pl.multiple_of(d * rows, rows), rows)
+    part = rows // 4
+
+    def own_part(d, k):
+        return gp.at[pl.ds(pl.multiple_of(d * rows + k * part, part), part), :]
 
     def arc(k, way):
         return half if (k + way) % 2 == 0 else half - 1
@@ -135,70 +172,122 @@
             for way in ways:
                 if half - arc(k, way) == s:
                     d = target(way, half - s)
-                    hop(gp.at[own_rows(d), column(k)], way, k, s).start()
+                    hop(own_part(d, k), way, k, s).start()
 
     def onward(s, k, way):
         held = zrecv.at[way, k, s - 1]
         hop(held, way, k, s - 1).wait_recv()
         d = target(way, half - s)
-        held[...] = (held[...].astype(F32) + gp[own_rows(d), column(k)].astype(F32)).astype(BF16)
+        held[...] = (held[...].astype(F32) + own_part(d, k)[...].astype(F32)).astype(BF16)
         hop(held, way, k, s).start()
 
     load.wait()
     third = hb // 3
 
-    pl.semaphore_wait(barrier, nb + 1)
-    begin(0, (0, 1))
-    begin(1, (0, 1))
-    spread(0, third)
-
+    @pl.when(first_plane)
+    def _():
+        pl.semaphore_wait(barrier, nb - 1)
+        spread(0, hb)
+        spread_diagonal()
+        for way in range(2):
+            pl.semaphore_wait(ready.at[way], 1)
+            begin(0, (way,))
+            begin(1, (way,))
+
+    @pl.when(jnp.logical_not(first_plane))
+    def _():
+        @pl.when(late)
+        def _():
+            pl.semaphore_wait(barrier, 7)
+
+        @pl.when(jnp.logical_not(late))
+        def _():
+            pl.semaphore_wait(barrier, nb + 1)
+
+        for way, neighbour in ((1, up), (0, down)):
+            @pl.when(neighbour == 0)
+            def _():
+                tell(ready.at[way], 0, me)
+
+        begin(0, (0, 1))
+        begin(1, (0, 1))
+
+        @pl.when(jnp.logical_not(late))
+        def _():
+            spread(0, third)
+
+    give(0)
+    take(0)
+    give(1)
     for k in range(4):
         for way in range(2):
             if arc(k, way) == half:
                 onward(1, k, way)
-
-    spread(third, 2 * third)
-
-    def all_onward(s):
-        for k in range(4):
+    take(1)
+    give(2)
+
+    early = jnp.logical_and(jnp.logical_not(late), jnp.logical_not(first_plane))
+
+    @pl.when(early)
+    def _():
+        spread(third, 2 * third)
+
+    def some_onward(s, low, high):
+        for k in range(low, high):
             for way in range(2):
                 onward(s, k, way)
 
     if half > 2:
-        all_onward(2)
-
-    spread(2 * third, hb)
-    spread_diagonal()
-
-    @pl.loop(3, half)
+        some_onward(2, 0, 2)
+    take(2)
+    give(3)
+    if half > 2:
+        some_onward(2, 2, 4)
+    take(3)
+
+    @pl.when(early)
+    def _():
+        spread(2 * third, hb)
+        spread_diagonal()
+
+    @pl.when(late)
+    def _():
+        spread(0, 2 * third)
+
+    if half > 3:
+        some_onward(3, 0, 4)
+
+    @pl.when(late)
+    def _():
+        spread(2 * third, hb)
+        spread_diagonal()
+
+    @pl.loop(4, half)
     def _(s):
-        all_onward(s)
-
-    for w in range(2):
-        parts = []
-        for k in (2 * w, 2 * w + 1):
-            for way in range(2):
-                hop(zrecv.at[way, k, half - 1], way, k, half - 1).wait_recv()
-            total = (gp[own_rows(z), column(k)].astype(F32) + zrecv[0, k, half - 1].astype(F32)
-                     + zrecv[1, k, half - 1].astype(F32))
-            parts.append(total.reshape(grp, 8, cw))
-        zstage[w] = jnp.concatenate(parts, axis=1).astype(BF16)
-
-        @pl.loop(0, grp)
-        def _(i):
-            j = peer_site(i)
+        some_onward(s, 0, 4)
+
+    few = grp // 4
+    for k in range(4):
+        total = own_part(z, k)[...].astype(F32)
+        for way in range(2):
+            hop(zrecv.at[way, k, half - 1], way, k, half - 1).wait_recv()
+            total = total + zrecv[way, k, half - 1].astype(F32)
+        halves = [total[:, h * 2 * cw:(h + 1) * 2 * cw].reshape(few, 8, 2 * cw) for h in range(2)]
+        zstage[pl.ds(k * few, few)] = jnp.concatenate(halves, axis=1).astype(BF16)
+
+        @pl.loop(k * few, (k + 1) * few)
+        def _(j):
             who = site_of(j)
 
             @pl.when(who != me)
             def _():
                 pltpu.make_async_remote_copy(
-                    src_ref=zstage.at[w, j], dst_ref=gbuf.at[w, me],
-                    send_sem=g_send.at[w], recv_sem=g_recv.at[w],
+                    src_ref=zstage.at[j], dst_ref=gbuf.at[me], send_sem=g_send, recv_sem=g_recv,
                     device_id=there(z, who), device_id_type=MESH).start()
 
-        @pl.when(is_site)
-        def _():
-            gbuf[w, me] = zstage[w, own_site]
+            @pl.when(who == me)
+            def _():
+                gbuf[me] = zstage[j]
 
     def settle(ref, sem):
         pltpu.make_async_copy(ref, ref, sem).wait()
@@ -224,13 +313,12 @@
 
     @pl.when(is_site)
     def _():
-        for w in range(2):
-            settle(gbuf.at[w, pl.ds(0, nb - 1)], g_recv.at[w])
-            pieces = gbuf[w].astype(F32).reshape(nb, 2, 8, cw)
-            for h in range(2):
-                piece = pieces[:, h].reshape(order, cw).astype(BF16)
-                g_ref[:, column(2 * w + h)] = piece
-                gt_ref[column(2 * w + h), :] = piece.T
+        settle(gbuf.at[pl.ds(0, nb - 1)], g_recv)
+        pieces = gbuf[...].astype(F32).reshape(nb, 2, 8, 2 * cw)
+        for h in range(2):
+            piece = pieces[:, h].reshape(order, 2 * cw).astype(BF16)
+            g_ref[:, h * 2 * cw:(h + 1) * 2 * cw] = piece
+            gt_ref[h * 2 * cw:(h + 1) * 2 * cw, :] = piece.T
         settle(diags.at[pl.ds(0, nb - 1)], d_recv)
         chosen = diags[table[own_site]]
         right_diag = jnp.concatenate([chosen[i:i + 1, :] for i in range(4)], axis=1)
@@ -318,15 +406,13 @@
     def _():
         settle(selbuf.at[pl.ds(0, grp - 1)], f_send)
         settle(diags.at[pl.ds(0, grp - 1)], d_send)
-        for w in range(2):
-            settle(zstage.at[w, pl.ds(0, grp - 1)], g_send.at[w])
+        settle(zstage.at[pl.ds(0, grp - 1)], g_send)
 
     @pl.when(jnp.logical_not(is_site))
     def _():
         settle(selbuf, f_send)
         settle(diags.at[pl.ds(0, grp)], d_send)
-        for w in range(2):
-            settle(zstage.at[w], g_send.at[w])
+        settle(zstage, g_send)
 
     for k in range(4):
         for way in range(2):
@@ -350,7 +436,7 @@
                   pl.BlockSpec(memory_space=pltpu.HBM), pl.BlockSpec(memory_space=pltpu.HBM)],
         out_specs=pl.BlockSpec(memory_space=pltpu.VMEM),
         scratch_shapes=[vmem((nz * rows, order), BF16), dma,
-            vmem((2, 4, half, rows, cw), BF16), vmem((2, grp, 16, cw), BF16), vmem((2, nb, 16, cw), BF16),
+            vmem((2, 4, half, rows // 4, order), BF16), vmem((grp, 16, 2 * cw), BF16), vmem((nb, 16, 2 * cw), BF16),
             vmem((order, order), BF16), vmem((order, order), BF16), vmem((2, order, 2 * cw), BF16),
             vmem((nb, 16, 2 * cw), BF16), vmem((grp, 16, 2 * cw), BF16), vmem((nb, 16, 2 * cw), BF16),
             vmem((order, order), BF16), vmem((order, order), BF16),
@@ -360,11 +446,12 @@
             vmem((order, order), BF16), vmem((order, order), BF16), vmem((order, order), BF16),
             vmem((order, order), BF16), vmem((order, order), BF16), vmem((order, order), BF16),
             vmem((nb, 16, 2 * cw), BF16), vmem((grp, 16, 2 * cw), BF16),
-            dma((2, 4, half)), dma((2, 4, half)), dma((2,)), dma((2,)),
+            dma((2, 4, half)), dma((2, 4, half)), dma, dma,
             dma, dma, dma, dma, dma, dma, dma, dma, dma, dma,
+            pltpu.SemaphoreType.REGULAR((2,)), pltpu.SemaphoreType.REGULAR((4,)),
         ],
         compiler_params=pltpu.CompilerParams(
-            collective_id=0, has_side_effects=True, vmem_limit_bytes=62 * 1024 * 1024),
+            collective_id=0, has_side_effects=True, vmem_limit_bytes=53 * 1024 * 1024 + 512 * 1024),
     )(owner_table, grad_part.reshape(nz * rows, order), left_stats[0, 0], right_stats[0, 0])
     return out.reshape(grp, 8, order)
 

time: 64.4 us -> 62.1 us (0.964)
  Pallas kernels: 62.6 us -> 60.6 us
    pallas_call x1, Pallas kernels: 62.6 us -> 60.6 us  [body(): pl.pallas_call(functools.partial(kernel, nz, nb, grp), out_shape=jax.Shap...]
    unnamed x1 -> x3, local copies, waits for them, and re-layouts: 1.57 us -> 1.31 us
where the time goes in v3:
time: 62.1 us; the launch traced here: 61.9 us
  Pallas kernels  60.6 us (98%)
  local copies, waits for them, and re-layouts  1.31 us (2%)
    pallas_call x1, Pallas kernels, body(): pl.pallas_call(functools.partial(kernel, nz, nb, grp), out_shape=jax.Shap...  60.6 us
    unnamed x3, local copies, waits for them, and re-layouts  1.31 us

profile of v3, /device:TPU:1, one launch (start us, length us, event | category | flops | bytes accessed | tf_op | source)
XLA Modules:
  0.0 61.9 jit_solution(10844795637607321932)
XLA Ops:
  0.0 0.0 copy-start
  0.0 0.7 %copy-done = s32[16]{0:T(128)S(1)} copy-done((s32[16]{0:T(128)S(1)}, s32[16]{0:T(128)}, u32[]{:S(2)}) %copy-start) | copy-done | bytes 88
  0.7 60.6 %shard_map.46 = bf16[128,512]{1,0:T(8,128)(2,1)S(1)} custom-call(s32[16]{0:T(128)S(1)} %copy-done, bf16[1536,512]{1,0:T(8,128)(2,1)} %bitcast.5, bf16[512,512]{1,0:T(8,128)(2,1)} %bitcast.6, bf16[512,512]{1,0:T(8,128)(2,1)} %bitcast.7), custom_call_target="tpu_custom_call" | custom-call | tf_op jit(solution)/shard_map/pallas_call | solution.py:432
  61.2 0.7 %copy.6 = bf16[16,8,512]{2,1,0:T(8,128)(2,1)} copy(bf16[16,8,512]{2,1,0:T(8,128)(2,1)S(1)} %bitcast.4) | data formatting | bytes 262144
Async XLA Ops:
  0.0 0.7 %copy-start = (s32[16]{0:T(128)S(1)}, s32[16]{0:T(128)}, u32[]{:S(2)}) copy-start(s32[16]{0:T(128)} %table.1) | copy-start | bytes 196

commit v4 on v3

--- a/solution.py
+++ b/solution.py
@@ -31,7 +31,7 @@
            diag, diags, g_ref, gt_ref,
            wide_l, wide_r, low_l, low_r, sq_l, sq_r, mix_l, mix_r, upd, rbuf,
            z_send, z_recv, g_send, g_recv, s_send, s_recv, f_send, f_recv, u_send, u_recv, d_send, d_recv,
-           l_sem, r_sem, ready, token):
+           l_sem, r_sem, token):
     z = lax.axis_index("dp")
     me = lax.axis_index("block")
     order = 8 * nb
@@ -73,7 +73,6 @@
     def moved(dy, dx, dc):
         return (lax.rem(y + dy + height, height) * width + lax.rem(x + dx + width, width)) * cores + lax.rem(c + dc, cores)
 
-    first_plane = z == 0
     late = z >= half
     barrier = pltpu.get_barrier_semaphore()
 
@@ -81,9 +80,7 @@
         pl.semaphore_signal(semaphore, inc=1, device_id=there(dp, block), device_id_type=MESH)
 
     for neighbour in (up, down):
-        @pl.when(neighbour != 0)
-        def _():
-            tell(barrier, neighbour, me)
+        tell(barrier, neighbour, me)
 
     @pl.when(late)
     def _():
@@ -110,6 +107,93 @@
         def _():
             if rounds[r]:
                 pl.semaphore_wait(token.at[r], len(rounds[r]))
+
+    def spread(low, high):
+        def act(d):
+            pltpu.make_async_remote_copy(
+                src_ref=pair.at[d // hb, pl.ds(pl.multiple_of(16 * lax.rem(d, hb), 16), 16)], dst_ref=statbuf.at[me],
+                send_sem=s_send, recv_sem=s_recv, device_id=there(z, d), device_id_type=MESH).start()
+
+        each_peer(low, high, act)
+
+    def spread_diagonal():
+        @pl.loop(0, grp)
+        def _(i):
+            who = site_of(peer_site(i))
+
+            @pl.when(who != me)
+            def _():
+                pltpu.make_async_remote_copy(
+                    src_ref=diag, dst_ref=diags.at[me], send_sem=d_send, recv_sem=d_recv,
+                    device_id=there(z, who), device_id_type=MESH).start()
+
+    part = rows // 4
+
+    def own_part(d, k, held=gp):
+        return held.at[pl.ds(pl.multiple_of(d * rows + k * part, part), part), :]
+
+    def arc(k, way):
+        return half if (k + way) % 2 == 0 else half - 1
+
+    def hop(src, way, k, s):
+        return pltpu.make_async_remote_copy(
+            src_ref=src, dst_ref=zrecv.at[way, k, s],
+            send_sem=z_send.at[way, k, s], recv_sem=z_recv.at[way, k, s],
+            device_id=there(up if way == 0 else down, me), device_id_type=MESH)
+
+    def target(way, dist):
+        return lax.rem(z + dist, nz) if way == 0 else lax.rem(z + nz - dist, nz)
+
+    def begin(s, ways):
+        for k in range(4):
+            for way in ways:
+                if half - arc(k, way) == s:
+                    d = target(way, half - s)
+                    hop(own_part(d, k, gp_hbm), way, k, s).start()
+
+    def onward(s, k, way):
+        held = zrecv.at[way, k, s - 1]
+        hop(held, way, k, s - 1).wait_recv()
+        d = target(way, half - s)
+        held[...] = (held[...].astype(F32) + own_part(d, k)[...].astype(F32)).astype(BF16)
+        hop(held, way, k, s).start()
+
+    def settle(ref, sem):
+        pltpu.make_async_copy(ref, ref, sem).wait()
+
+    def relay():
+        settle(statbuf.at[pl.ds(0, nb - 1)], s_recv)
+
+        @pl.loop(0, grp)
+        def _(i):
+            j = peer_site(i)
+            selbuf[j] = statbuf[table[j]]
+            who = site_of(j)
+
+            @pl.when(who != me)
+            def _():
+                pltpu.make_async_remote_copy(
+                    src_ref=selbuf.at[j], dst_ref=statfull.at[me],
+                    send_sem=f_send, recv_sem=f_recv,
+                    device_id=there(z, who), device_id_type=MESH).start()
+
+        @pl.when(is_site)
+        def _():
+            statfull[me] = selbuf[own_site]
+
+    third = hb // 3
+
+    @pl.when(late)
+    def _():
+        pl.semaphore_wait(barrier, 7)
+
+    @pl.when(jnp.logical_not(late))
+    def _():
+        pl.semaphore_wait(barrier, nb + 1)
+
+    begin(0, (0, 1))
+    begin(1, (0, 1))
+    give(0)
 
     load_l.wait()
     load_r.wait()
@@ -131,92 +215,12 @@
     def _():
         diags[me] = diag[...]
 
-    def spread(low, high):
-        def act(d):
-            pltpu.make_async_remote_copy(
-                src_ref=pair.at[d // hb, pl.ds(pl.multiple_of(16 * lax.rem(d, hb), 16), 16)], dst_ref=statbuf.at[me],
-                send_sem=s_send, recv_sem=s_recv, device_id=there(z, d), device_id_type=MESH).start()
-
-        each_peer(low, high, act)
-
-    def spread_diagonal():
-        @pl.loop(0, grp)
-        def _(i):
-            who = site_of(peer_site(i))
-
-            @pl.when(who != me)
-            def _():
-                pltpu.make_async_remote_copy(
-                    src_ref=diag, dst_ref=diags.at[me], send_sem=d_send, recv_sem=d_recv,
-                    device_id=there(z, who), device_id_type=MESH).start()
-
-    part = rows // 4
-
-    def own_part(d, k):
-        return gp.at[pl.ds(pl.multiple_of(d * rows + k * part, part), part), :]
-
-    def arc(k, way):
-        return half if (k + way) % 2 == 0 else half - 1
-
-    def hop(src, way, k, s):
-        return pltpu.make_async_remote_copy(
-            src_ref=src, dst_ref=zrecv.at[way, k, s],
-            send_sem=z_send.at[way, k, s], recv_sem=z_recv.at[way, k, s],
-            device_id=there(up if way == 0 else down, me), device_id_type=MESH)
-
-    def target(way, dist):
-        return lax.rem(z + dist, nz) if way == 0 else lax.rem(z + nz - dist, nz)
-
-    def begin(s, ways):
-        for k in range(4):
-            for way in ways:
-                if half - arc(k, way) == s:
-                    d = target(way, half - s)
-                    hop(own_part(d, k), way, k, s).start()
-
-    def onward(s, k, way):
-        held = zrecv.at[way, k, s - 1]
-        hop(held, way, k, s - 1).wait_recv()
-        d = target(way, half - s)
-        held[...] = (held[...].astype(F32) + own_part(d, k)[...].astype(F32)).astype(BF16)
-        hop(held, way, k, s).start()
-
-    load.wait()
-    third = hb // 3
-
-    @pl.when(first_plane)
-    def _():
-        pl.semaphore_wait(barrier, nb - 1)
+    @pl.when(jnp.logical_not(late))
+    def _():
         spread(0, hb)
         spread_diagonal()
-        for way in range(2):
-            pl.semaphore_wait(ready.at[way], 1)
-            begin(0, (way,))
-            begin(1, (way,))
-
-    @pl.when(jnp.logical_not(first_plane))
-    def _():
-        @pl.when(late)
-        def _():
-            pl.semaphore_wait(barrier, 7)
-
-        @pl.when(jnp.logical_not(late))
-        def _():
-            pl.semaphore_wait(barrier, nb + 1)
-
-        for way, neighbour in ((1, up), (0, down)):
-            @pl.when(neighbour == 0)
-            def _():
-                tell(ready.at[way], 0, me)
-
-        begin(0, (0, 1))
-        begin(1, (0, 1))
-
-        @pl.when(jnp.logical_not(late))
-        def _():
-            spread(0, third)
-
-    give(0)
+
+    load.wait()
     take(0)
     give(1)
     for k in range(4):
@@ -226,12 +230,6 @@
     take(1)
     give(2)
 
-    early = jnp.logical_and(jnp.logical_not(late), jnp.logical_not(first_plane))
-
-    @pl.when(early)
-    def _():
-        spread(third, 2 * third)
-
     def some_onward(s, low, high):
         for k in range(low, high):
             for way in range(2):
@@ -245,26 +243,28 @@
         some_onward(2, 2, 4)
     take(3)
 
-    @pl.when(early)
+    @pl.when(late)
+    def _():
+        spread(0, 2 * third)
+
+    if half > 3:
+        some_onward(3, 0, 4)
+
+    @pl.when(late)
     def _():
         spread(2 * third, hb)
         spread_diagonal()
 
-    @pl.when(late)
-    def _():
-        spread(0, 2 * third)
-
-    if half > 3:
-        some_onward(3, 0, 4)
-
-    @pl.when(late)
-    def _():
-        spread(2 * third, hb)
-        spread_diagonal()
-
-    @pl.loop(4, half)
+    @pl.loop(4, half - 1)
     def _(s):
         some_onward(s, 0, 4)
+
+    @pl.when(jnp.logical_not(late))
+    def _():
+        relay()
+
+    if half > 4:
+        some_onward(half - 1, 0, 4)
 
     few = grp // 4
     for k in range(4):
@@ -289,36 +289,12 @@
             def _():
                 gbuf[me] = zstage[j]
 
-    def settle(ref, sem):
-        pltpu.make_async_copy(ref, ref, sem).wait()
-
-    settle(statbuf.at[pl.ds(0, nb - 1)], s_recv)
-
-    @pl.loop(0, grp)
-    def _(i):
-        j = peer_site(i)
-        selbuf[j] = statbuf[table[j]]
-        who = site_of(j)
-
-        @pl.when(who != me)
-        def _():
-            pltpu.make_async_remote_copy(
-                src_ref=selbuf.at[j], dst_ref=statfull.at[me],
-                send_sem=f_send, recv_sem=f_recv,
-                device_id=there(z, who), device_id_type=MESH).start()
+    @pl.when(late)
+    def _():
+        relay()
 
     @pl.when(is_site)
     def _():
-        statfull[me] = selbuf[own_site]
-
-    @pl.when(is_site)
-    def _():
-        settle(gbuf.at[pl.ds(0, nb - 1)], g_recv)
-        pieces = gbuf[...].astype(F32).reshape(nb, 2, 8, 2 * cw)
-        for h in range(2):
-            piece = pieces[:, h].reshape(order, 2 * cw).astype(BF16)
-            g_ref[:, h * 2 * cw:(h + 1) * 2 * cw] = piece
-            gt_ref[h * 2 * cw:(h + 1) * 2 * cw, :] = piece.T
         settle(diags.at[pl.ds(0, nb - 1)], d_recv)
         chosen = diags[table[own_site]]
         right_diag = jnp.concatenate([chosen[i:i + 1, :] for i in range(4)], axis=1)
@@ -330,18 +306,24 @@
         nr = 2
         rb = order // nr
         blocks = [pl.ds(i * rb, rb) for i in range(nr)]
+        for i, rs in enumerate(blocks):
+            row = lax.broadcasted_iota(jnp.int32, (rb, order), 0) + i * rb
+            col = lax.broadcasted_iota(jnp.int32, (rb, order), 1)
+            stored, turned = m_ref[rs, :].astype(F32), mt_ref[rs, :].astype(F32)
+            wide_l[rs, :] = DECAY * jnp.where(col >= row, stored, turned)
+            wide_r[rs, :] = DECAY * jnp.where(col == row, right_diag, jnp.where(col > row, turned, stored))
+        settle(gbuf.at[pl.ds(0, nb - 1)], g_recv)
+        pieces = gbuf[...].astype(F32).reshape(nb, 2, 8, 2 * cw)
+        for h in range(2):
+            piece = pieces[:, h].reshape(order, 2 * cw).astype(BF16)
+            g_ref[:, h * 2 * cw:(h + 1) * 2 * cw] = piece
+            gt_ref[h * 2 * cw:(h + 1) * 2 * cw, :] = piece.T
         sides = ((0, g_ref, gt_ref, wide_l, low_l, sq_l, mix_l), (1, gt_ref, g_ref, wide_r, low_r, sq_r, mix_r))
         bounds = []
         for side, a, b, wide, low, sq, mix in sides:
             sums = jnp.zeros((1, order), F32)
             for i, rs in enumerate(blocks):
-                row = lax.broadcasted_iota(jnp.int32, (rb, order), 0) + i * rb
-                col = lax.broadcasted_iota(jnp.int32, (rb, order), 1)
-                above, below = (m_ref, mt_ref) if side == 0 else (mt_ref, m_ref)
-                prev = jnp.where(col >= row, above[rs, :].astype(F32), below[rs, :].astype(F32))
-                if side == 1:
-                    prev = jnp.where(col == row, right_diag, prev)
-                stat = DECAY * prev + (1.0 - DECAY) * wide_dot(a[rs, :], b[...], ((1,), (0,)))
+                stat = wide[rs, :] + (1.0 - DECAY) * wide_dot(a[rs, :], b[...], ((1,), (0,)))
                 wide[rs, :] = stat
                 sums = sums + jnp.sum(jnp.abs(stat), axis=0, keepdims=True)
             bounds.append(jnp.max(sums, axis=1, keepdims=True))
@@ -448,7 +430,7 @@
             vmem((nb, 16, 2 * cw), BF16), vmem((grp, 16, 2 * cw), BF16),
             dma((2, 4, half)), dma((2, 4, half)), dma, dma,
             dma, dma, dma, dma, dma, dma, dma, dma, dma, dma,
-            pltpu.SemaphoreType.REGULAR((2,)), pltpu.SemaphoreType.REGULAR((4,)),
+            pltpu.SemaphoreType.REGULAR((4,)),
         ],
         compiler_params=pltpu.CompilerParams(
             collective_id=0, has_side_effects=True, vmem_limit_bytes=53 * 1024 * 1024 + 512 * 1024),

time: 62.1 us -> 59.7 us (0.961)
  Pallas kernels: 60.6 us -> 58.3 us
    pallas_call x1, Pallas kernels: 60.6 us -> 58.3 us  [body(): pl.pallas_call(functools.partial(kernel, nz, nb, grp), out_shape=jax.Shap...]
where the time goes in v4:
time: 59.7 us; the launch traced here: 59.6 us
  Pallas kernels  58.3 us (98%)
  local copies, waits for them, and re-layouts  1.31 us (2%)
    pallas_call x1, Pallas kernels, body(): pl.pallas_call(functools.partial(kernel, nz, nb, grp), out_shape=jax.Shap...  58.3 us
    unnamed x3, local copies, waits for them, and re-layouts  1.31 us

profile of v4, /device:TPU:1, one launch (start us, length us, event | category | flops | bytes accessed | tf_op | source)
XLA Modules:
  0.0 59.6 jit_solution(6449979705496222919)
XLA Ops:
  0.0 0.0 copy-start
  0.0 0.7 %copy-done = s32[16]{0:T(128)S(1)} copy-done((s32[16]{0:T(128)S(1)}, s32[16]{0:T(128)}, u32[]{:S(2)}) %copy-start) | copy-done | bytes 88
  0.7 58.3 %shard_map.46 = bf16[128,512]{1,0:T(8,128)(2,1)S(1)} custom-call(s32[16]{0:T(128)S(1)} %copy-done, bf16[1536,512]{1,0:T(8,128)(2,1)} %bitcast.5, bf16[512,512]{1,0:T(8,128)(2,1)} %bitcast.6, bf16[512,512]{1,0:T(8,128)(2,1)} %bitcast.7), custom_call_target="tpu_custom_call" | custom-call | tf_op jit(solution)/shard_map/pallas_call | solution.py:414
  58.9 0.7 %copy.6 = bf16[16,8,512]{2,1,0:T(8,128)(2,1)} copy(bf16[16,8,512]{2,1,0:T(8,128)(2,1)S(1)} %bitcast.4) | data formatting | bytes 262144
Async XLA Ops:
  0.0 0.7 %copy-start = (s32[16]{0:T(128)S(1)}, s32[16]{0:T(128)}, u32[]{:S(2)}) copy-start(s32[16]{0:T(128)} %table.1) | copy-start | bytes 196

commit v5 on v4

--- a/solution.py
+++ b/solution.py
@@ -12,10 +12,6 @@
 MESH = pl.DeviceIdType.MESH
 F32 = jnp.float32
 BF16 = jnp.bfloat16
-
-
-def site_of(j):
-    return 4 * j + 2 * lax.rem(j // 2, 2) + 1
 
 
 def zigzag(i, n):
@@ -38,7 +34,16 @@
     cw = order // 4
     rows = grp * 8
     half = nz // 2
-    own_site = me // 4
+    few = grp // 4
+
+    def site_of(j):
+        place = 4 * lax.rem(j, few) + j // few
+        return 4 * place + 2 * lax.rem(place // 2, 2) + 1
+
+    def block_at(place):
+        return lax.rem(place, 4) * few + place // 4
+
+    own_site = block_at(me // 4)
     is_site = me == site_of(own_site)
 
     def there(dp, block):
@@ -64,7 +69,7 @@
             act(lax.rem(me + (hb - i), nb))
 
     def peer_site(i):
-        return lax.rem(own_site + zigzag(i, grp), grp)
+        return block_at(lax.rem(me // 4 + zigzag(i, grp), grp))
 
     cores, width = 2, 4
     height = nb // (cores * width)
@@ -266,7 +271,6 @@
     if half > 4:
         some_onward(half - 1, 0, 4)
 
-    few = grp // 4
     for k in range(4):
         total = own_part(z, k)[...].astype(F32)
         for way in range(2):

time: 59.7 us -> 59.6 us (level)
  no operation moved by 1% of the time
where the time goes in v5:
time: 59.6 us; the launch traced here: 59.4 us
  Pallas kernels  58.1 us (97%)
  local copies, waits for them, and re-layouts  1.31 us (2%)
    pallas_call x1, Pallas kernels, body(): pl.pallas_call(functools.partial(kernel, nz, nb, grp), out_shape=jax.Shap...  58.1 us
    unnamed x3, local copies, waits for them, and re-layouts  1.31 us

profile of v5, /device:TPU:1, one launch (start us, length us, event | category | flops | bytes accessed | tf_op | source)
XLA Modules:
  0.0 59.4 jit_solution(5494502280249009128)
XLA Ops:
  0.0 0.0 copy-start
  0.0 0.7 %copy-done = s32[16]{0:T(128)S(1)} copy-done((s32[16]{0:T(128)S(1)}, s32[16]{0:T(128)}, u32[]{:S(2)}) %copy-start) | copy-done | bytes 88
  0.7 58.1 %shard_map.46 = bf16[128,512]{1,0:T(8,128)(2,1)S(1)} custom-call(s32[16]{0:T(128)S(1)} %copy-done, bf16[1536,512]{1,0:T(8,128)(2,1)} %bitcast.5, bf16[512,512]{1,0:T(8,128)(2,1)} %bitcast.6, bf16[512,512]{1,0:T(8,128)(2,1)} %bitcast.7), custom_call_target="tpu_custom_call" | custom-call | tf_op jit(solution)/shard_map/pallas_call | solution.py:418
  58.8 0.7 %copy.6 = bf16[16,8,512]{2,1,0:T(8,128)(2,1)} copy(bf16[16,8,512]{2,1,0:T(8,128)(2,1)S(1)} %bitcast.4) | data formatting | bytes 262144
Async XLA Ops:
  0.0 0.7 %copy-start = (s32[16]{0:T(128)S(1)}, s32[16]{0:T(128)}, u32[]{:S(2)}) copy-start(s32[16]{0:T(128)} %table.1) | copy-start | bytes 196
